TPU v7x, 256 devices: a whole 4x4x8 slice. The times are simulated.
256 devices in a mesh: group: 8 (over x, core), dev: 32 (over z, y).
Axes of the slice: x: 4, y: 4, z: 8, core: 2. Of those that a mesh axis runs over, the one named last changes fastest.
Arguments:
- features: bfloat16 [1048576, 128], P(('group', 'dev')), may hold values from -6 to 6
- coords: bfloat16 [3, 1048576], P(None, ('group', 'dev')), may hold values from 0 to 1
- near_pairs: int32 [2, 8192], P(None, 'group'), may hold values from 0 to 511, as said below
- parent_two: int32 [4096], P(('group', 'dev')), may hold values from 0 to 127, as said below
- parent_three: int32 [1024], P('group'), may hold values from 0 to 7
- rates: float32 [4], replicated, may hold values from 6 to 40
- w_near: bfloat16 [128, 128], replicated, may hold values from -0.5 to 0.5
- restrict: bfloat16 [64, 256], replicated, may hold values from -0.375 to 0.375
- w_two: bfloat16 [128, 128], replicated, may hold values from -0.5 to 0.5
- w_three: bfloat16 [128, 128], replicated, may hold values from -0.5 to 0.5
- w_four: bfloat16 [128, 128], replicated, may hold values from -0.5 to 0.5
- coupling: bfloat16 [64, 64], replicated, may hold values from -0.75 to 0.75
- expand: bfloat16 [256, 64], replicated, may hold values from -0.75 to 0.75
- w_out: bfloat16 [128, 128], replicated, may hold values from -0.5 to 0.5
Outputs:
- mixed: bfloat16 [1048576, 128], P(('group', 'dev'))
Inputs may be any that keep to these rules, and one draw needn't show every extreme that they name: `near_pairs`: for any two devices A and P of dev in one region, at most 2 near pairs of that region have their first block on A and their second on P, and in each region some such two devices have exactly 2. `parent_two`: every level-two node of a region is named by exactly four blocks of that region.
All inputs are finite; a program needn't handle non-finite values.
Results may differ from a plain program's by a relative error of at most 0.008.
Values may be sent and summed in bfloat16 or wider, within the bound.
No kernel may reach another device: no remote copies, remote signals or barrier semaphores. Data moves between devices by JAX's collectives and lax.ppermute only.
A program may use at most 128 MiB of HBM per device.

v0:
```python
import jax
import jax.numpy as jnp
from jax import lax
from jax.sharding import Mesh
from jax.sharding import PartitionSpec as P

CAP = 2
NODES3_GROUP = 8
DEV = ("dev_0", "dev_1")
GROUP_DEV = ("group", "dev_0", "dev_1")


def in_blocks(array, dim, peers):
    before, after = (array.shape[:dim], array.shape[dim + 1 :])
    return jnp.moveaxis(array.reshape(*before, peers, -1, *after), dim, 0)


def summed_on_arrival(array, axis, dim):
    peers = lax.axis_size(axis)
    pieces = lax.all_to_all(in_blocks(array, dim, peers), axis, 0, 0, tiled=True)
    return jnp.sum(pieces, axis=0)


def by_axis(array, axes):
    for axis in axes:
        array = lax.psum(array, axis)
    return array


def sent_to_all(array, axis):
    copies = jnp.broadcast_to(array, (lax.axis_size(axis), *array.shape))
    return lax.all_to_all(copies, axis, split_axis=0, concat_axis=0, tiled=True)


def in_order(pieces, dim):
    shape = list(pieces.shape[1:])
    shape[dim] *= pieces.shape[0]
    return jnp.moveaxis(pieces, 0, dim).reshape(shape)


def gathered_copies(array, axis, dim):
    pieces = sent_to_all(array, axis)
    return in_order(pieces, dim)


def kernel_table(cloud_one, cloud_two, rates):
    first_pos = cloud_one.astype(jnp.float32)
    second_pos = cloud_two.astype(jnp.float32)
    delta_x = first_pos[:, 0, :, None] - second_pos[:, 0, None, :]
    delta_y = first_pos[:, 1, :, None] - second_pos[:, 1, None, :]
    delta_z = first_pos[:, 2, :, None] - second_pos[:, 2, None, :]
    distance = delta_x * delta_x + delta_y * delta_y + delta_z * delta_z
    return jnp.exp(-rates[None, :, None, None] * distance[:, None]).astype(jnp.bfloat16)


def apply_table(kernel, block_values, head_count):
    channels = block_values.shape[-1]
    head_of = jnp.arange(channels, dtype=jnp.int32) // (channels // head_count)
    head_mask = (head_of[None, :] == jnp.arange(head_count, dtype=jnp.int32)[:, None]).astype(
        jnp.bfloat16
    )
    masked = block_values[:, None, :, :] * head_mask[None, :, None, :]
    form = "nhpq,nhqc->npc"
    return jnp.einsum(form, kernel, masked, preferred_element_type=jnp.float32)


def in_groups(array):
    return array.reshape((array.shape[0] // 8, 8) + array.shape[1:])


def per_device(
    features,
    coords,
    near_pairs,
    parent_two,
    parent_three,
    rates,
    w_near,
    restrict,
    w_two,
    w_three,
    w_four,
    coupling,
    expand,
    w_out,
):
    dev_count = lax.axis_size(DEV)
    dev_index = lax.axis_index(DEV)
    group_index = lax.axis_index("group")
    points_n, channels = features.shape
    blk_points = expand.shape[0]
    summary_rows = expand.shape[1]
    block_count = points_n // blk_points
    head_count = rates.shape[0]
    block_range = jnp.arange(block_count, dtype=jnp.int32)
    values = jnp.dot(features, w_near, preferred_element_type=jnp.float32).astype(jnp.bfloat16)
    vblocks = values.reshape(block_count, blk_points, channels)
    cblocks = coords.reshape(3, block_count, blk_points).transpose(1, 0, 2)

    def self_term(operands):
        cloud, block_values = operands
        return apply_table(kernel_table(cloud, cloud, rates), block_values, head_count)

    near_field = lax.map(
        self_term,
        (cblocks.reshape(-1, 4, 3, blk_points), vblocks.reshape(-1, 4, blk_points, channels)),
    )
    near_field = near_field.reshape(block_count, blk_points * channels)
    first_block = near_pairs[0]
    second_block = near_pairs[1]
    owner_first = first_block // block_count
    owner_second = second_block // block_count
    pair_key = owner_first * dev_count + owner_second
    position = jnp.arange(first_block.shape[0], dtype=jnp.int32)
    slot_rank = jnp.sum(
        (pair_key[:, None] == pair_key[None, :]) & (position[None, :] < position[:, None]), axis=1
    )
    slot_rows = dev_count * CAP
    row_range = jnp.arange(slot_rows, dtype=jnp.int32)
    peer_of_row = row_range // CAP
    slot_of_row = row_range % CAP
    same_slot = slot_rank[None, :] == slot_of_row[:, None]
    match_first = (
        (owner_first[None, :] == dev_index)
        & (owner_second[None, :] == peer_of_row[:, None])
        & same_slot
    )
    match_second = (
        (owner_first[None, :] == peer_of_row[:, None])
        & (owner_second[None, :] == dev_index)
        & same_slot
    )
    live_first = jnp.any(match_first, axis=1)
    live_second = jnp.any(match_second, axis=1)
    index_first = jnp.sum(jnp.where(match_first, first_block[None, :] % block_count, 0), axis=1)
    index_second = jnp.sum(jnp.where(match_second, second_block[None, :] % block_count, 0), axis=1)

    def pick_blocks(index, live_rows):
        weight = live_rows.astype(jnp.bfloat16)
        picked_values = (vblocks[index] * weight[:, None, None]).reshape(
            dev_count, CAP, blk_points, channels
        )
        picked_coords = (cblocks[index] * weight[:, None, None]).reshape(
            dev_count, CAP, 3, blk_points
        )
        return (picked_values, picked_coords)

    send_values, send_coords = pick_blocks(index_second, live_second)
    mine_coords = cblocks[index_first]
    onehot_second = ((index_second[None, :] == block_range[:, None]) & live_second[None, :]).astype(
        jnp.bfloat16
    )

    def accumulate(running, side, index, live_rows):
        flat_side = side.reshape(side.shape[0], -1) * live_rows[:, None]
        return running.at[index].add(flat_side)

    back_values, back_coords = pick_blocks(index_first, live_first)
    got_values, got_coords, other_values, other_coords = (
        lax.all_to_all(send_values, DEV, split_axis=0, concat_axis=0, tiled=True),
        lax.all_to_all(send_coords, DEV, split_axis=0, concat_axis=0, tiled=True),
        lax.all_to_all(back_values, DEV, split_axis=0, concat_axis=0, tiled=True),
        lax.all_to_all(back_coords, DEV, split_axis=0, concat_axis=0, tiled=True),
    )
    got_values = got_values.reshape(slot_rows, blk_points, channels)
    got_coords = got_coords.reshape(slot_rows, 3, blk_points)
    other_values = other_values.reshape(slot_rows, blk_points, channels)
    other_coords = other_coords.reshape(slot_rows, 3, blk_points)

    def first_step(running, operands):
        first_pos, second_pos, second_vals, index, live_rows = operands
        side_first = apply_table(
            kernel_table(first_pos, second_pos, rates), second_vals, head_count
        )
        return (accumulate(running, side_first, index, live_rows), None)

    def second_step(running, operands):
        own_pos, partner_pos, partner_vals, onehot = operands
        side_second = apply_table(
            kernel_table(own_pos, partner_pos, rates), partner_vals, head_count
        ).astype(jnp.bfloat16)
        return (
            running
            + jnp.dot(
                onehot,
                side_second.reshape(side_second.shape[0], -1),
                preferred_element_type=jnp.float32,
            ),
            None,
        )

    near_field, _ = lax.scan(
        first_step,
        near_field,
        (
            in_groups(mine_coords),
            in_groups(got_coords),
            in_groups(got_values),
            in_groups(index_first),
            in_groups(live_first.astype(jnp.float32)),
        ),
    )
    onehot_grouped = onehot_second.reshape(block_count, slot_rows // 8, 8).transpose(1, 0, 2)
    near_field, _ = lax.scan(
        second_step,
        near_field,
        (
            in_groups(cblocks[index_second]),
            in_groups(other_coords),
            in_groups(other_values),
            onehot_grouped,
        ),
    )
    level_one = jnp.einsum(
        "sb,nbc->nsc",
        restrict,
        features.reshape(block_count, blk_points, channels),
        preferred_element_type=jnp.float32,
    )
    level_one = level_one.astype(jnp.bfloat16).reshape(block_count, summary_rows * channels)
    nodes_group = parent_three.shape[0]
    per_dev = nodes_group // dev_count
    coarse_range = jnp.arange(NODES3_GROUP, dtype=jnp.int32)
    coarse_scale = NODES3_GROUP / nodes_group
    select = (
        parent_two[None, :] == jnp.arange(per_dev * lax.axis_size(DEV), dtype=jnp.int32)[:, None]
    ).astype(jnp.bfloat16)
    flat = (
        summed_on_arrival(jnp.dot(select, level_one, preferred_element_type=jnp.float32), DEV, 0)
        .astype(jnp.bfloat16)
        .reshape(-1, channels)
    )
    result = jax.nn.gelu(jnp.dot(flat, w_two, preferred_element_type=jnp.float32)).astype(
        jnp.bfloat16
    )
    level_two = result.reshape(-1, summary_rows * channels)
    mine_three = lax.dynamic_slice_in_dim(parent_three, dev_index * per_dev, per_dev)
    select = (mine_three[None, :] == coarse_range[:, None]).astype(jnp.bfloat16)
    level_three = by_axis(jnp.dot(select, level_two, preferred_element_type=jnp.float32), DEV)
    level_three = (level_three * coarse_scale).astype(jnp.bfloat16)
    three_all = gathered_copies(level_three, "group", 0)
    coupling_rows = lax.dynamic_slice_in_dim(coupling, group_index * NODES3_GROUP, NODES3_GROUP, 0)
    mixed_three = jnp.dot(coupling_rows, three_all, preferred_element_type=jnp.float32).astype(
        jnp.bfloat16
    )
    down_three = jax.nn.gelu(
        jnp.dot(mixed_three.reshape(-1, channels), w_three, preferred_element_type=jnp.float32)
    )
    down_three = down_three.astype(jnp.bfloat16).reshape(NODES3_GROUP, summary_rows * channels)
    lift_table = (mine_three[:, None] == coarse_range[None, :]).astype(jnp.bfloat16)
    lifted = jnp.dot(
        level_two.reshape(-1, channels), w_four, preferred_element_type=jnp.float32
    ).reshape(-1, summary_rows * channels)
    down_two = jax.nn.gelu(
        lifted + jnp.dot(lift_table, down_three, preferred_element_type=jnp.float32)
    ).astype(jnp.bfloat16)
    shard_rows = gathered_copies(down_two, DEV, 0)
    select = (
        parent_two[:, None] == jnp.arange(shard_rows.shape[0], dtype=jnp.int32)[None, :]
    ).astype(jnp.bfloat16)
    parent_down = jnp.dot(select, shard_rows, preferred_element_type=jnp.float32).astype(
        jnp.bfloat16
    )
    far_field = jnp.einsum(
        "bs,nsc->nbc",
        expand,
        parent_down.reshape(block_count, summary_rows, channels),
        preferred_element_type=jnp.float32,
    )
    far_field = far_field.astype(jnp.bfloat16).reshape(points_n, channels)
    total = near_field.reshape(points_n, channels) * blk_points ** (-0.5) + jnp.dot(
        far_field, w_out, preferred_element_type=jnp.float32
    )
    return total.astype(jnp.bfloat16)


def solution(mesh):
    torus = Mesh(mesh.devices.reshape(mesh.shape["group"], 8, 4), ("group", "dev_0", "dev_1"))
    in_specs = (
        P(GROUP_DEV, None),
        P(None, GROUP_DEV),
        P(None, "group"),
        P(GROUP_DEV),
        P("group"),
        P(),
        P(),
        P(),
        P(),
        P(),
        P(),
        P(),
        P(),
        P(),
    )
    out_specs = P(GROUP_DEV, None)
    return jax.shard_map(
        per_device, mesh=torus, in_specs=in_specs, out_specs=out_specs, check_vma=False
    )
```

profile of v0, /device:TPU:6, one launch (start us, length us, event | category | flops | bytes accessed | tf_op | source)
XLA Modules:
  0.0 478.9 jit_solution(13457422486970932100)
XLA Ops:
  11.8 11.5 %all-to-all-start = ((bf16[32,2,3,256]{3,1,2,0:T(2,128)(2,1)}), bf16[32,2,3,256]{3,1,2,0:T(2,128)(2,1)S(1)}, u32[]{:S(2)}, u32[]{:S(2)}) async-start(bf16[32,2,3,256]{3,1,2,0:T(2,128)(2,1)} %copy_multiply_fusion.1), calls=%async_computation | async-start | bytes 196608 | tf_op jit(solution)/shard_map/all_to_all | solution.py:161
  26.9 6.6 %all-to-all-done = bf16[32,2,3,256]{3,1,2,0:T(2,128)(2,1)S(1)} async-done(((bf16[32,2,3,256]{3,1,2,0:T(2,128)(2,1)}), bf16[32,2,3,256]{3,1,2,0:T(2,128)(2,1)S(1)}, u32[]{:S(2)}, u32[]{:S(2)}) %all-to-all-start) | async-done | bytes 98336 | tf_op jit(solution)/shard_map/all_to_all | solution.py:161
  33.5 3.8 all-to-all-start.2
  38.2 4.7 copy.52
  42.9 4.8 all-to-all-done.2
  47.6 5.2 %all-to-all-start.4 = ((f32[32,4,8192]{2,1,0:T(4,128)}), f32[32,4,8192]{2,1,0:T(4,128)}, u32[]{:S(2)}, u32[]{:S(2)}) async-start(f32[32,4,8192]{2,1,0:T(4,128)} %copy.52), calls=%async_computation.4 | async-start | bytes 8388608 | tf_op jit(solution)/shard_map/all_to_all | solution.py:20
  53.3 3.0 gather_fusion.2
  56.3 4.5 broadcast_multiply_fusion.1
  60.8 84.8 %all-to-all-done.4 = f32[32,4,8192]{2,1,0:T(4,128)} async-done(((f32[32,4,8192]{2,1,0:T(4,128)}), f32[32,4,8192]{2,1,0:T(4,128)}, u32[]{:S(2)}, u32[]{:S(2)}) %all-to-all-start.4) | async-done | bytes 4194336 | tf_op jit(solution)/shard_map/all_to_all | solution.py:20
  145.6 6.8 %all-to-all-start.1 = ((bf16[32,2,256,128]{3,2,1,0:T(8,128)(2,1)}), bf16[32,2,256,128]{3,2,1,0:T(8,128)(2,1)}, u32[]{:S(2)}, u32[]{:S(2)}) async-start(bf16[32,2,256,128]{3,2,1,0:T(8,128)(2,1)} %broadcast_multiply_fusion.1), calls=%async_computation.1 | async-start | bytes 8388608 | tf_op jit(solution)/shard_map/all_to_all | solution.py:160
  152.5 3.0 gather_fusion.3
  155.6 8.8 %while.36 = (s32[]{:T(128)}, f32[4,4,256,128]{3,2,1,0:T(8,128)}, f32[1,4,1,1]{1,3,2,0:T(1,128)S(1)}, bf16[4,4,3,256]{3,1,2,0:T(4,128)(2,1)S(1)}, bf16[4,4,256,128]{3,2,1,0:T(8,128)(2,1)S(1)}, /*index=5*/s32[]{:T(128)}) while((s32[]{:T(128)}, f32[4,4,256,128]{3,2,1,0:T(8,128)}, f32[1,4,1,1]{1,3,2,0:T(1,128)S(1)}, ...), condition=%wide.region_1.2_spmd, body=%wide.region_0.1_spmd.sunk | while | flops 273159168 | bytes 3466845 | solution.py:104
  165.0 2.9 reduce_sum.45
  169.3 4.5 broadcast_multiply_fusion
  176.0 2.8 copy.77
  180.4 76.3 %all-reduce.3.cloned.1.call-done = f32[8,8192]{1,0:T(8,128)} async-done(((f32[8,8192]{1,0:T(8,128)}), f32[8,8192]{1,0:T(8,128)}) %all-reduce.3.cloned.1.call-update) | async-done | bytes 262160 | tf_op jit(solution)/shard_map/psum | solution.py:26
  256.8 8.0 %all-to-all-start.3 = ((bf16[32,2,256,128]{3,2,1,0:T(8,128)(2,1)}), bf16[32,2,256,128]{3,2,1,0:T(8,128)(2,1)}, u32[]{:S(2)}, u32[]{:S(2)}) async-start(bf16[32,2,256,128]{3,2,1,0:T(8,128)(2,1)} %broadcast_multiply_fusion), calls=%async_computation.3 | async-start | bytes 8388608 | tf_op jit(solution)/shard_map/all_to_all | solution.py:162
  264.8 75.2 %while.37 = (s32[]{:T(128)}, f32[16,32768]{1,0:T(8,128)S(1)}, s32[8,8]{1,0:T(8,128)}, f32[1,4,1,1]{1,3,2,0:T(1,128)S(1)}, bf16[8,8,3,256]{3,1,2,0:T(8,128)(2,1)}...) while((s32[]{:T(128)}, f32[16,32768]{1,0:T(8,128)S(1)}, ...), condition=%wide.region_9.10_spmd, body=%wide.region_7.9_spmd.sunk | while | flops 546846720 | bytes 12283201 | solution.py:192
  271.7 2.5 scatter_fusion
  281.1 2.5 scatter_fusion
  299.9 2.5 scatter_fusion
  309.3 2.5 scatter_fusion
  318.7 2.5 scatter_fusion
  328.1 2.5 scatter_fusion
  341.0 16.7 %all-to-all-done.3 = bf16[32,2,256,128]{3,2,1,0:T(8,128)(2,1)} async-done(((bf16[32,2,256,128]{3,2,1,0:T(8,128)(2,1)}), bf16[32,2,256,128]{3,2,1,0:T(8,128)(2,1)}, u32[]{:S(2)}, u32[]{:S(2)}) %all-to-all-start.3) | async-done | bytes 4194336 | tf_op jit(solution)/shard_map/all_to_all | solution.py:162
  358.7 5.1 %all-to-all-start.5 = ((bf16[8,8,8192]{2,1,0:T(8,128)(2,1)}), bf16[8,8,8192]{2,1,0:T(8,128)(2,1)}, u32[]{:S(2)}, u32[]{:S(2)}) async-start(bf16[8,8,8192]{2,1,0:T(8,128)(2,1)} %broadcast_in_dim.47), calls=%async_computation.5 | async-start | bytes 2097152 | tf_op jit(solution)/shard_map/all_to_all | solution.py:32
  363.8 39.9 %while.38 = (s32[]{:T(128)}, f32[16,32768]{1,0:T(8,128)S(1)}, bf16[8,16,8]{1,2,0:T(8,128)(2,1)S(1)}, f32[1,4,1,1]{1,3,2,0:T(1,128)S(1)}, bf16[8,8,3,256]{3,1,2,0...) while((s32[]{:T(128)}, f32[16,32768]{1,0:T(8,128)S(1)}, ...), condition=%wide.region_11.12_spmd, body=%wide.region_10.11_spmd.sunk | while | flops 555497472 | bytes 11236469 | solution.py:204
  408.5 5.3 %all-to-all-start.6 = ((bf16[32,4,8192]{2,1,0:T(4,128)(2,1)}), bf16[32,4,8192]{2,1,0:T(4,128)(2,1)}, u32[]{:S(2)}, u32[]{:S(2)}) async-start(bf16[32,4,8192]{2,1,0:T(4,128)(2,1)} %broadcast_in_dim.48), calls=%async_computation.6 | async-start | bytes 4194304 | tf_op jit(solution)/shard_map/all_to_all | solution.py:32
  415.2 2.7 mul.430
  418.0 46.2 %all-to-all-done.6 = bf16[32,4,8192]{2,1,0:T(4,128)(2,1)} async-done(((bf16[32,4,8192]{2,1,0:T(4,128)(2,1)}), bf16[32,4,8192]{2,1,0:T(4,128)(2,1)}, u32[]{:S(2)}, u32[]{:S(2)}) %all-to-all-start.6) | async-done | bytes 2097184 | tf_op jit(solution)/shard_map/all_to_all | solution.py:32
  464.2 2.5 reshape.467
  469.3 2.7 fusion.43
  (293 shorter events, 134.5 us)
Async XLA Ops:
  6.5 18.4 %copy-start = (bf16[4096,128]{1,0:T(8,128)(2,1)S(1)}, bf16[4096,128]{1,0:T(8,128)(2,1)}, u32[]{:S(2)}) copy-start(bf16[4096,128]{1,0:T(8,128)(2,1)} %param.20) | copy-start | bytes 3145732
  6.5 30.8 %copy-start.8 = (s32[16]{0:T(128)S(1)}, s32[16]{0:T(128)}, u32[]{:S(2)}) copy-start(s32[16]{0:T(128)} %param.23) | copy-start | bytes 196
  11.8 21.7 %all-to-all-start = ((bf16[32,2,3,256]{3,1,2,0:T(2,128)(2,1)}), bf16[32,2,3,256]{3,1,2,0:T(2,128)(2,1)S(1)}, u32[]{:S(2)}, u32[]{:S(2)}) async-start(bf16[32,2,3,256]{3,1,2,0:T(2,128)(2,1)} %copy_multiply_fusion.1), calls=%async_computation | async-start | bytes 196608 | tf_op jit(solution)/shard_map/all_to_all | solution.py:161
  33.5 14.1 %all-to-all-start.2 = ((bf16[32,2,3,256]{3,1,2,0:T(2,128)(2,1)}), bf16[32,2,3,256]{3,1,2,0:T(2,128)(2,1)S(1)}, u32[]{:S(2)}, u32[]{:S(2)}) async-start(bf16[32,2,3,256]{3,1,2,0:T(2,128)(2,1)} %copy_multiply_fusion), calls=%async_computation.2 | async-start | bytes 196608 | tf_op jit(solution)/shard_map/all_to_all | solution.py:163
  42.9 10.0 %copy-start.4 = (bf16[128,128]{1,0:T(8,128)(2,1)S(1)}, bf16[128,128]{1,0:T(8,128)(2,1)}, u32[]{:S(2)}) copy-start(bf16[128,128]{1,0:T(8,128)(2,1)} %param.26) | copy-start | bytes 98308
  47.6 98.0 %all-to-all-start.4 = ((f32[32,4,8192]{2,1,0:T(4,128)}), f32[32,4,8192]{2,1,0:T(4,128)}, u32[]{:S(2)}, u32[]{:S(2)}) async-start(f32[32,4,8192]{2,1,0:T(4,128)} %copy.52), calls=%async_computation.4 | async-start | bytes 8388608 | tf_op jit(solution)/shard_map/all_to_all | solution.py:20
  145.6 111.2 %all-to-all-start.1 = ((bf16[32,2,256,128]{3,2,1,0:T(8,128)(2,1)}), bf16[32,2,256,128]{3,2,1,0:T(8,128)(2,1)}, u32[]{:S(2)}, u32[]{:S(2)}) async-start(bf16[32,2,256,128]{3,2,1,0:T(8,128)(2,1)} %broadcast_multiply_fusion.1), calls=%async_computation.1 | async-start | bytes 8388608 | tf_op jit(solution)/shard_map/all_to_all | solution.py:160
  152.4 104.4 %all-reduce.3.cloned.1.call-start = ((), (), s32[]{:S(2)}) async-start(), calls=%async_computation.7 | async-start | bytes 524288 | tf_op jit(solution)/shard_map/psum | solution.py:26
  152.5 3.0 copy-start.3
  152.5 3.1 copy-start.14
  152.5 3.1 copy-start.15
  155.6 12.6 %copy-start.10 = (s32[4]{0:T(128)}, s32[4]{0:T(128)S(1)}, u32[]{:S(2)}) copy-start(s32[4]{0:T(128)S(1)} %dynamic_slice.79) | copy-start | bytes 52
  164.4 0.6 copy-start.16
  165.0 3.0 copy-start.12
  169.1 170.9 %all-reduce.5.cloned.1.call-start = ((), (), s32[]{:S(2)}) async-start(), calls=%async_computation.8 | async-start | bytes 524288 | tf_op jit(solution)/shard_map/psum | solution.py:26
  256.8 8.0 %copy-start.17 = (f32[1,4,1,1]{1,3,2,0:T(1,128)S(1)}, f32[1,4,1,1]{1,3,2,0:T(1,128)}, u32[]{:S(2)}) copy-start(f32[1,4,1,1]{1,3,2,0:T(1,128)} %copy-done.16) | copy-start | bytes 52
  256.8 100.9 %all-to-all-start.3 = ((bf16[32,2,256,128]{3,2,1,0:T(8,128)(2,1)}), bf16[32,2,256,128]{3,2,1,0:T(8,128)(2,1)}, u32[]{:S(2)}, u32[]{:S(2)}) async-start(bf16[32,2,256,128]{3,2,1,0:T(8,128)(2,1)} %broadcast_multiply_fusion), calls=%async_computation.3 | async-start | bytes 8388608 | tf_op jit(solution)/shard_map/all_to_all | solution.py:162
  358.7 45.2 %all-to-all-start.5 = ((bf16[8,8,8192]{2,1,0:T(8,128)(2,1)}), bf16[8,8,8192]{2,1,0:T(8,128)(2,1)}, u32[]{:S(2)}, u32[]{:S(2)}) async-start(bf16[8,8,8192]{2,1,0:T(8,128)(2,1)} %broadcast_in_dim.47), calls=%async_computation.5 | async-start | bytes 2097152 | tf_op jit(solution)/shard_map/all_to_all | solution.py:32
  363.8 39.9 %copy-start.6 = (bf16[128,128]{1,0:T(8,128)(2,1)S(1)}, bf16[128,128]{1,0:T(8,128)(2,1)}, u32[]{:S(2)}) copy-start(bf16[128,128]{1,0:T(8,128)(2,1)} %param.30) | copy-start | bytes 98308
  363.8 41.7 %copy-start.13 = (bf16[128,128]{1,0:T(8,128)(2,1)S(1)}, bf16[128,128]{1,0:T(8,128)(2,1)}, u32[]{:S(2)}) copy-start(bf16[128,128]{1,0:T(8,128)(2,1)} %param.29) | copy-start | bytes 98308
  403.7 2.1 copy-start.11
  408.5 55.7 %all-to-all-start.6 = ((bf16[32,4,8192]{2,1,0:T(4,128)(2,1)}), bf16[32,4,8192]{2,1,0:T(4,128)(2,1)}, u32[]{:S(2)}, u32[]{:S(2)}) async-start(bf16[32,4,8192]{2,1,0:T(4,128)(2,1)} %broadcast_in_dim.48), calls=%async_computation.6 | async-start | bytes 4194304 | tf_op jit(solution)/shard_map/all_to_all | solution.py:32
  417.9 48.8 %copy-start.9 = (s32[16]{0:T(128)S(1)}, s32[16]{0:T(128)}, u32[]{:S(2)}) copy-start(s32[16]{0:T(128)} %param.23) | copy-start | bytes 196
  466.8 0.8 copy-start.7
  467.2 2.1 copy-start.2
  467.2 2.1 copy-start.5
  469.3 2.7 copy-start.1
Sparse Core Ops, SparseCore 0:
  169.2 87.4 all-reduce.2
  259.2 54.4 all-reduce.4
where the time goes:
time: 482 us; the launch traced here: 479 us
  waiting for transfers between devices  236 us (49%)
  other arithmetic  81.6 us (17%)
  local copies, waits for them, and re-layouts  55.5 us (12%)
  starting transfers between devices  45.9 us (10%)
  matrix products  45.2 us (9%)
  between operations  13.9 us (3%)
    all_to_all x1, waiting for transfers between devices, summed_on_arrival(): lax.all_to_all(in_blocks(array, dim, peers), axis, 0, 0, tiled=True)  84.8 us
    psum x2, waiting for transfers between devices, by_axis(): array = lax.psum(array, axis)  76.4 us
    all_to_all x2, waiting for transfers between devices, sent_to_all(): return lax.all_to_all(copies, axis, split_axis=0, concat_axis=0, tiled=True)  46.2 us
    dot_general x20, matrix products, apply_table(): return jnp.einsum(form, kernel, masked, preferred_element_type=jnp.float32)  30.4 us
    scatter-add x8, other arithmetic, accumulate(): return running.at[index].add(flat_side)  19.7 us
    mul x20, local copies, waits for them, and re-layouts, apply_table(): masked = block_values[:, None, :, :] * head_mask[None, :, None, :]  17.4 us
    all_to_all x1, waiting for transfers between devices, per_device(): lax.all_to_all(back_values, DEV, split_axis=0, concat_axis=0, tiled=True)  16.7 us
    add x20, other arithmetic, kernel_table(): distance = delta_x * delta_x + delta_y * delta_y + delta_z * delta_z  16 us
  transfers between devices with their start and end apart: 9, of which 6 were waited for; matrix products, arithmetic and copies ran while one was open for 34% of the time, Pallas kernels for 0%

commit v1 on v0

v1 whole, which is shorter than its diff:
```python
import functools
import math

import jax
import jax.numpy as jnp
from jax import lax
from jax.experimental import pallas as pl
from jax.experimental.pallas import tpu as pltpu
from jax.sharding import Mesh
from jax.sharding import PartitionSpec as P

NODES3_GROUP = 8
DEV = ("dev_0", "dev_1")
GROUP_DEV = ("group", "dev_0", "dev_1")
F32 = jnp.float32
BF16 = jnp.bfloat16
ROWS = 8
COLS = 4
BLK = 16
RBLK = BLK * COLS
B = 256
HC = 32
AUG = 16
UNROLL = 8
VMEM_LIMIT = 48 << 20


def dot_t(a, b, dims):
    return lax.dot_general(a, b, (dims, ((), ())), preferred_element_type=F32)


def vmem():
    return pl.BlockSpec(memory_space=pltpu.VMEM)


def smem():
    return pl.BlockSpec(memory_space=pltpu.SMEM)


def params():
    return pltpu.CompilerParams(vmem_limit_bytes=VMEM_LIMIT)


def prep_kernel(f_ref, wn_ref, re_ref, v_ref, lev_ref):
    for i in range(4):
        f = f_ref[i * B : (i + 1) * B, :]
        v = dot_t(wn_ref[...], f, ((0,), (1,))).astype(BF16)
        v_ref[:, i] = v.reshape(COLS, HC, B)
        lev_ref[i] = jnp.dot(re_ref[...], f, preferred_element_type=F32).astype(BF16)


def prep(features, w_near, restrict):
    return pl.pallas_call(
        prep_kernel,
        grid=(BLK // 4,),
        in_specs=[
            pl.BlockSpec((4 * B, 128), lambda i: (i, 0)),
            pl.BlockSpec((128, 128), lambda i: (0, 0)),
            pl.BlockSpec((64, B), lambda i: (0, 0)),
        ],
        out_specs=[
            pl.BlockSpec((COLS, 4, HC, B), lambda i: (0, i, 0, 0)),
            pl.BlockSpec((4, 64, 128), lambda i: (i, 0, 0)),
        ],
        out_shape=[
            jax.ShapeDtypeStruct((COLS, BLK, HC, B), BF16),
            jax.ShapeDtypeStruct((BLK, 64, 128), BF16),
        ],
        compiler_params=params(),
        name="prep",
    )(features, w_near, restrict)


def pieces(x):
    one = x.astype(BF16).astype(F32)
    rest = x - one
    two = rest.astype(BF16).astype(F32)
    three = (rest - two).astype(BF16).astype(F32)
    return (one, two, three)


def stacked(rows, width):
    at = lax.broadcasted_iota(jnp.int32, (AUG, width), 0)
    out = jnp.zeros((AUG, width), F32)
    for k, row in enumerate(rows):
        out = jnp.where(at == k, row, out)
    return out.astype(BF16)


def aug_kernel(z_ref, c_ref, xyz_ref, src_ref, dst_ref):
    scale = c_ref[0]
    width = BLK * B
    ones = [jnp.ones((1, width), F32)] * 3
    for y in range(COLS):
        xyz = xyz_ref[y, 0].astype(F32)
        axes = [xyz[k : k + 1] for k in range(3)]
        norm = pieces(-scale * (axes[0] * axes[0] + axes[1] * axes[1] + axes[2] * axes[2]))
        src = stacked(axes * 3 + ones + list(norm), width)
        for b in range(BLK):
            src_ref[0, y * BLK + b] = src[:, b * B : (b + 1) * B]

        @pl.when(pl.program_id(0) == 0)
        def _():
            turned = [pieces(2.0 * scale * a) for a in axes]
            rows = [turned[k][i] for i in range(3) for k in range(3)]
            dst = stacked(rows + list(norm) + ones, width)
            for b in range(BLK):
                dst_ref[y * BLK + b] = dst[:, b * B : (b + 1) * B]


def augment(z, scale, placed):
    return pl.pallas_call(
        aug_kernel,
        grid_spec=pltpu.PrefetchScalarGridSpec(
            num_scalar_prefetch=1,
            grid=(ROWS,),
            in_specs=[
                pl.BlockSpec(memory_space=pltpu.SMEM),
                pl.BlockSpec((COLS, 1, 4, BLK * B), lambda d, z: (0, lax.rem(z[0] + d, ROWS), 0, 0)),
            ],
            out_specs=[
                pl.BlockSpec((1, RBLK, AUG, B), lambda d, z: (d, 0, 0, 0)),
                pl.BlockSpec((RBLK, AUG, B), lambda d, z: (0, 0, 0)),
            ],
        ),
        out_shape=[
            jax.ShapeDtypeStruct((ROWS, RBLK, AUG, B), BF16),
            jax.ShapeDtypeStruct((RBLK, AUG, B), BF16),
        ],
        compiler_params=params(),
        name="augment",
    )(z, scale, placed)


def self_kernel(scale_ref, xyz_ref, v_ref, out_ref):
    ones = [jnp.ones((1, B), F32)] * 3
    for i in range(4):
        xyz = xyz_ref[:, i * B : (i + 1) * B].astype(F32)
        axes = [xyz[k : k + 1] for k in range(3)]
        norm = list(pieces(-(axes[0] * axes[0] + axes[1] * axes[1] + axes[2] * axes[2])))
        src = stacked(axes + ones + norm, B)
        dst = stacked([2.0 * a for a in axes] + norm + ones, B)
        power = dot_t(dst, src, ((0,), (0,)))
        for h in range(COLS):
            table = jnp.exp2(power * scale_ref[h]).astype(BF16)
            out_ref[h, i] = dot_t(v_ref[h, i], table, ((1,), (1,)))


def self_near(scales, coords, values):
    block = pl.BlockSpec((COLS, 4, HC, B), lambda i: (0, i, 0, 0))
    return pl.pallas_call(
        self_kernel,
        grid=(BLK // 4,),
        in_specs=[smem(), pl.BlockSpec((3, 4 * B), lambda i: (0, i)), block],
        out_specs=block,
        out_shape=jax.ShapeDtypeStruct((COLS, BLK, HC, B), F32),
        compiler_params=params(),
        cost_estimate=pl.CostEstimate(
            flops=64 * 2 * B * B * 256, bytes_accessed=3 << 20, transcendentals=64 * B * B
        ),
        name="self",
    )(scales, coords, values)


def near_kernel(parts, first, last, cnt, lst, dst_ref, *refs):
    n = len(parts)
    v_refs, s_refs = refs[:n], refs[n : 2 * n]
    if last:
        acc, out = refs[-2:]
    else:
        acc = refs[-1]
    if first:
        acc[...] = jnp.zeros_like(acc)
    for (row, offset), v_ref, s_ref in zip(parts, v_refs, s_refs):

        def body(i, carry):
            done = []
            for u in range(UNROLL):
                code = lst[row, i * UNROLL + u]
                dst = code >> 6
                src = code & 63
                power = dot_t(dst_ref[jnp.minimum(dst, RBLK - 1)], s_ref[0, src], ((0,), (0,)))
                table = jnp.exp2(power).astype(BF16)
                done.append((dst, dot_t(v_ref[src - offset], table, ((1,), (1,)))))
            for dst, term in done:
                acc[dst] += term
            return carry

        lax.fori_loop(0, (cnt[row] + UNROLL - 1) // UNROLL, body, 0)
    if last:
        out[...] = acc[:RBLK].astype(BF16)


def near_step(cnt, lst, dst_aug, src_aug, parts, chunks, acc, last=False):
    first = acc is None
    acc_shape = (RBLK + 1, HC, B)
    row_spec = [
        pl.BlockSpec((1, RBLK, AUG, B), functools.partial(lambda r, i: (r, 0, 0, 0), r))
        for _, r, _ in parts
    ]
    whole = lambda shape: pl.BlockSpec(shape, lambda i: (0,) * len(shape))
    in_specs = [smem(), smem(), whole(dst_aug.shape)]
    in_specs += [whole(c.shape) for c in chunks] + row_spec
    args = [cnt, lst, dst_aug, *chunks, *([src_aug] * len(parts))]
    if not first:
        in_specs.append(vmem())
        args.append(acc)
    sides = 36 * len(parts)
    shapes = [jax.ShapeDtypeStruct(acc_shape, F32)]
    if last:
        shapes.append(jax.ShapeDtypeStruct((RBLK, HC, B), BF16))
    return pl.pallas_call(
        functools.partial(near_kernel, tuple((p, o) for p, _, o in parts), first, last),
        grid=(1,),
        in_specs=in_specs,
        out_specs=[vmem()] * len(shapes),
        out_shape=shapes,
        input_output_aliases={} if first else {len(args) - 1: 0},
        compiler_params=params(),
        cost_estimate=pl.CostEstimate(
            flops=sides * 2 * B * B * 256, bytes_accessed=8 << 20, transcendentals=sides * B * B
        ),
        name="near",
    )(*args)[-1]


def side_lists(near_pairs, z):
    dst = jnp.concatenate([near_pairs[0], near_pairs[1]])
    src = jnp.concatenate([near_pairs[1], near_pairs[0]])
    n = dst.shape[0]
    rel = jnp.remainder(src // RBLK - z, ROWS)
    kind = jnp.where((rel == 4) & (src % RBLK >= RBLK // 2), ROWS, rel)
    kind = jnp.where(dst // RBLK == z, kind, -1)
    kinds = ROWS + 1
    hit = kind[None, :] == jnp.arange(kinds, dtype=jnp.int32)[:, None]
    cells = hit.reshape(kinds, n // 128, 128).astype(BF16)
    lane = jnp.arange(128, dtype=jnp.int32)
    upto = (lane[:, None] < lane[None, :]).astype(BF16)
    within = jnp.einsum("kab,bc->kac", cells, upto, preferred_element_type=F32)
    total = jnp.sum(cells.astype(F32), axis=2)
    chunk = jnp.arange(n // 128, dtype=jnp.int32)
    before = jnp.sum(
        jnp.where(chunk[None, None, :] < chunk[None, :, None], total[:, None, :], 0.0), axis=2
    )
    rank = (within + before[:, :, None]).astype(jnp.int32).reshape(kinds, n)
    rank = jnp.where(hit, rank, -1)
    code = (dst % RBLK) * RBLK + src % RBLK
    place = jnp.arange(RBLK, dtype=jnp.int32)
    lists = jnp.sum(
        jnp.where(rank[:, None, :] == place[None, :, None], code[None, None, :], 0), axis=2
    )
    count = jnp.sum(hit.astype(jnp.int32), axis=1)
    spare = RBLK * RBLK + jnp.where(jnp.arange(kinds) == ROWS, RBLK // 2, 0)
    lists = jnp.where(place[None, :] < count[:, None], lists, spare[:, None])
    return count.astype(jnp.int32), lists


def final_kernel(self_ref, near_ref, pd_ref, ex_ref, wo_ref, out_ref):
    row = lax.broadcasted_iota(jnp.int32, (128, 128), 0)
    col = lax.broadcasted_iota(jnp.int32, (128, 128), 1)
    turn = jnp.where(row == col, B ** (-0.5), 0.0).astype(BF16)
    for i in range(4):
        near = (self_ref[:, i] + near_ref[:, i].astype(F32)).reshape(128, B).astype(BF16)
        far = jnp.dot(ex_ref[...], pd_ref[i], preferred_element_type=F32).astype(BF16)
        total = dot_t(near, turn, ((0,), (0,))) + jnp.dot(
            far, wo_ref[...], preferred_element_type=F32
        )
        out_ref[i * B : (i + 1) * B, :] = total.astype(BF16)


def final(own, near, parent_down, expand, w_out):
    return pl.pallas_call(
        final_kernel,
        grid=(BLK // 4,),
        in_specs=[
            pl.BlockSpec((COLS, 4, HC, B), lambda i: (0, i, 0, 0)),
            pl.BlockSpec((COLS, 4, HC, B), lambda i: (0, i, 0, 0)),
            pl.BlockSpec((4, 64, 128), lambda i: (i, 0, 0)),
            pl.BlockSpec((B, 64), lambda i: (0, 0)),
            pl.BlockSpec((128, 128), lambda i: (0, 0)),
        ],
        out_specs=pl.BlockSpec((4 * B, 128), lambda i: (i, 0)),
        out_shape=jax.ShapeDtypeStruct((BLK * B, 128), BF16),
        compiler_params=params(),
        name="final",
    )(own, near, parent_down, expand, w_out)


def copies(array, axis):
    sent = jnp.broadcast_to(array, (lax.axis_size(axis), *array.shape))
    return lax.all_to_all(sent, axis, 0, 0, tiled=True)


def far_levels(level_one, parents, parent_three, w_two, w_three, w_four, coupling):
    channels = w_two.shape[0]
    nodes = parent_three.shape[0]
    peers = ROWS * COLS
    sent = level_one.reshape(BLK, peers, 2, channels).transpose(1, 0, 2, 3)
    sent = sent.reshape(peers, BLK, 2 * channels)
    rows = lax.all_to_all(sent, DEV, 0, 0, tiled=True).reshape(peers * BLK, 2 * channels)
    select = (jnp.arange(nodes, dtype=jnp.int32)[:, None] == parents[None, :]).astype(BF16)
    level_sum = jnp.dot(select, rows, preferred_element_type=F32).astype(BF16)

    def by_channel(array, weight):
        return jnp.dot(array.reshape(-1, channels), weight, preferred_element_type=F32)

    level_two = jax.nn.gelu(by_channel(level_sum, w_two)).astype(BF16).reshape(nodes, -1)
    coarse = jnp.arange(NODES3_GROUP, dtype=jnp.int32)
    select_three = (coarse[:, None] == parent_three[None, :]).astype(BF16)
    level_three = jnp.dot(select_three, level_two, preferred_element_type=F32)
    level_three = (level_three * (NODES3_GROUP / nodes)).astype(BF16)
    three_all = copies(level_three, "group").reshape(-1, level_three.shape[1])
    mine = lax.axis_index("group") * NODES3_GROUP
    coupling_rows = lax.dynamic_slice_in_dim(coupling, mine, NODES3_GROUP, 0)
    mixed = jnp.dot(coupling_rows, three_all, preferred_element_type=F32).astype(BF16)
    down_three = jax.nn.gelu(by_channel(mixed, w_three)).astype(BF16).reshape(NODES3_GROUP, -1)
    lift = (parent_three[:, None] == coarse[None, :]).astype(BF16)
    lifted = by_channel(level_two, w_four).reshape(nodes, -1)
    down_two = jax.nn.gelu(lifted + jnp.dot(lift, down_three, preferred_element_type=F32))
    down_two = down_two.astype(BF16)
    spread = (parents[:, None] == jnp.arange(nodes, dtype=jnp.int32)[None, :]).astype(BF16)
    down = jnp.dot(spread, down_two, preferred_element_type=F32).astype(BF16)
    back = lax.all_to_all(down.reshape(peers, BLK, -1), DEV, 0, 0, tiled=True)
    return back.reshape(peers, BLK, 2, channels).transpose(1, 0, 2, 3).reshape(BLK, -1, channels)


def per_device(
    features,
    coords,
    near_pairs,
    parent_two,
    parent_three,
    rates,
    w_near,
    restrict,
    w_two,
    w_three,
    w_four,
    coupling,
    expand,
    w_out,
):
    z = lax.axis_index("dev_0").astype(jnp.int32)
    y = lax.axis_index("dev_1").astype(jnp.int32)
    values, level_one = prep(features, w_near, restrict)
    held = lax.all_to_all(values, "dev_1", 0, 0, tiled=True).reshape(RBLK, HC, B)
    parent_row = jnp.pad(parent_two.astype(BF16), (0, coords.shape[1] - BLK))
    placed = jnp.concatenate([coords, parent_row[None, :]])
    placed = copies(placed, "dev_0")
    scales = rates * math.log2(math.e)
    own = self_near(scales, coords, values)
    held, placed, own = lax.optimization_barrier((held, placed, own))
    placed = copies(placed, "dev_1")
    parents = placed[:, :, 3, :BLK].transpose(1, 0, 2).reshape(-1).astype(jnp.int32)
    scale = jnp.sum(jnp.where(jnp.arange(COLS) == y, scales, 0.0)).reshape(1)
    src_aug, dst_aug = augment(z.reshape(1), scale, placed)
    cnt, lst = side_lists(near_pairs, z)
    parent_down = far_levels(level_one, parents, parent_three, w_two, w_three, w_four, coupling)

    up = [(i, (i + 1) % ROWS) for i in range(ROWS)]
    down = [(i, (i - 1) % ROWS) for i in range(ROWS)]
    step = functools.partial(near_step, cnt, lst, dst_aug, src_aug)
    acc = step([(0, 0, 0)], [held], None)
    below, above = held, held
    for d in range(1, 4):
        below = lax.ppermute(below, "dev_0", up)
        above = lax.ppermute(above, "dev_0", down)
        below, above, acc = lax.optimization_barrier((below, above, acc))
        acc = step([(ROWS - d, ROWS - d, 0), (d, d, 0)], [below, above], acc)
    half = RBLK // 2
    below = lax.ppermute(below[:half], "dev_0", up)
    above = lax.ppermute(above[half:], "dev_0", down)
    near = step([(4, 4, 0), (ROWS, 4, half)], [below, above], acc, last=True)
    near = lax.all_to_all(near.reshape(COLS, BLK, HC, B), "dev_1", 0, 0, tiled=True)
    return final(own, near, parent_down, expand, w_out)


def solution(mesh):
    torus = Mesh(mesh.devices.reshape(mesh.shape["group"], ROWS, COLS), GROUP_DEV)
    in_specs = (
        P(GROUP_DEV, None),
        P(None, GROUP_DEV),
        P(None, "group"),
        P(GROUP_DEV),
        P("group"),
        P(),
        P(),
        P(),
        P(),
        P(),
        P(),
        P(),
        P(),
        P(),
    )
    out_specs = P(GROUP_DEV, None)
    return jax.shard_map(
        per_device, mesh=torus, in_specs=in_specs, out_specs=out_specs, check_vma=False
    )
```

time: 482 us -> 196 us (0.41)
  waiting for transfers between devices: 236 us -> 55.2 us
  other arithmetic: 81.6 us -> 4.04 us
  Pallas kernels: 0 us -> 56.1 us
  matrix products: 45.2 us -> 2.87 us
  local copies, waits for them, and re-layouts: 55.5 us -> 18.6 us
  between operations: 13.9 us -> 0.37 us
  starting transfers between devices: 45.9 us -> 55.4 us
    all_to_all x7, waiting for transfers between devices: 159 us -> 54.7 us  [the longest x3 19.8 us: copies(): return lax.all_to_all(sent, axis, 0, 0, tiled=True)]
    psum x2 -> x0, waiting for transfers between devices: 76.4 us -> none  [by_axis(): array = lax.psum(array, axis)]
    pallas_call x0 -> x9, Pallas kernels: none -> 56.1 us  [the longest x5 35.6 us: near_step(): pl.pallas_call(functools.partial(near_kernel, tuple(((p, o) for p, _, o i...]
    dot_general x40 -> x8, matrix products: 45.2 us -> 2.87 us  [the longest x1 1.16 us: far_levels(): down = jnp.dot(spread, down_two, preferred_element_type=F32).astype(BF16)]
    mul x29 -> x0, local copies, waits for them, and re-layouts: 25.6 us -> none  [the longest x20 17.4 us: apply_table(): masked = block_values[:, None, :, :] * head_mask[None, :, None, :]]
    scatter-add x8 -> x0, other arithmetic: 19.7 us -> none  [accumulate(): return running.at[index].add(flat_side)]
    mul x13 -> x0, other arithmetic: 17 us -> none  [the longest x2 9.01 us: pick_blocks(): vblocks[index] * weight[:, None, None]]
    convert_element_type x60 -> x2, other arithmetic: 18.4 us -> 1.46 us  [the longest x1 0.79 us: per_device(): placed[:, :, 3, :BLK].transpose(1, 0, 2).reshape(-1).astype(jnp.int32)]
  transfers between devices with their start and end apart: 9 -> 15, of which waited for: 6 -> 7; matrix products, arithmetic and copies ran while one was open for 34% -> 6% of each run, Pallas kernels for 0% -> 27%
where the time goes in v1:
time: 196 us; the launch traced here: 193 us
  Pallas kernels  56.1 us (29%)
  starting transfers between devices  55.4 us (28%)
  waiting for transfers between devices  55.2 us (28%)
  local copies, waits for them, and re-layouts  18.6 us (9%)
  other arithmetic  4.04 us (2%)
  matrix products  2.87 us (1%)
    pallas_call x5, Pallas kernels, near_step(): pl.pallas_call(functools.partial(near_kernel, tuple(((p, o) for p, _, o i...  35.6 us
    all_to_all x3, waiting for transfers between devices, copies(): return lax.all_to_all(sent, axis, 0, 0, tiled=True)  19.8 us
    all_to_all x1, waiting for transfers between devices, far_levels(): lax.all_to_all(sent, DEV, 0, 0, tiled=True)  18.1 us
    all_to_all x3, starting transfers between devices, copies(): return lax.all_to_all(sent, axis, 0, 0, tiled=True)  16.5 us
    all_to_all x1, waiting for transfers between devices, per_device(): lax.all_to_all(near.reshape(COLS, BLK, HC, B), 'dev_1', 0, 0, tiled=True)  12.9 us
    all_to_all x1, starting transfers between devices, far_levels(): back = lax.all_to_all(down.reshape(peers, BLK, -1), DEV, 0, 0, tiled=True)  9.36 us
    ppermute x3, starting transfers between devices, per_device(): below = lax.ppermute(below, 'dev_0', up)  8.98 us
    unnamed x33, local copies, waits for them, and re-layouts  7.97 us
  transfers between devices with their start and end apart: 15, of which 7 were waited for; matrix products, arithmetic and copies ran while one was open for 6% of the time, Pallas kernels for 27%

profile of v1, /device:TPU:6, one launch (start us, length us, event | category | flops | bytes accessed | tf_op | source)
XLA Modules:
  0.0 192.6 jit_solution(2309100147352830081)
XLA Ops:
  2.3 8.5 %all-to-all-start.1 = ((bf16[8,4,4096]{2,1,0:T(4,128)(2,1)}), bf16[8,4,4096]{2,1,0:T(4,128)(2,1)S(1)}, u32[]{:S(2)}, u32[]{:S(2)}) async-start(bf16[8,4,4096]{2,1,0:T(4,128)(2,1)} %broadcast_in_dim.95), calls=%async_computation.1 | async-start | bytes 524288 | tf_op jit(solution)/shard_map/all_to_all | solution.py:291
  13.5 2.3 %prep.1 = (bf16[4,16,32,256]{3,2,1,0:T(8,128)(2,1)}, bf16[16,64,128]{2,1,0:T(8,128)(2,1)S(1)}) custom-call(bf16[4096,128]{1,0:T(8,128)(2,1)S(1)} %copy-done.5, bf16[128,128]{1,0:T(8,128)(2,1)S(1)} %copy-done.8, bf16[64,256]{1,0:T(8,128)(2,1)S(1)} %copy-done.9), custom_call_target="tpu_custom_call" | custom-call | tf_op jit(solution)/shard_map/prep/pallas_call | solution.py:53
  16.7 6.0 %all-to-all-done.1 = bf16[8,4,4096]{2,1,0:T(4,128)(2,1)S(1)} async-done(((bf16[8,4,4096]{2,1,0:T(4,128)(2,1)}), bf16[8,4,4096]{2,1,0:T(4,128)(2,1)S(1)}, u32[]{:S(2)}, u32[]{:S(2)}) %all-to-all-start.1) | async-done | bytes 262176 | tf_op jit(solution)/shard_map/all_to_all | solution.py:291
  22.7 4.5 %all-to-all-start = ((bf16[4,16,32,256]{3,2,1,0:T(8,128)(2,1)}), bf16[4,16,32,256]{3,2,1,0:T(8,128)(2,1)}, u32[]{:S(2)}, u32[]{:S(2)}) async-start(bf16[4,16,32,256]{3,2,1,0:T(8,128)(2,1)} %get-tuple-element.22.v_ref), calls=%async_computation | async-start | bytes 2097152 | tf_op jit(solution)/shard_map/all_to_all | solution.py:346
  28.0 7.3 %self.1.self_ref = f32[4,16,32,256]{3,2,1,0:T(8,128)S(1)} custom-call(f32[4]{0:T(128)S(1)} %get-tuple-element.48.scale_ref, bf16[3,4096]{1,0:T(4,128)(2,1)S(1)} %copy-done.10, bf16[4,16,32,256]{3,2,1,0:T(8,128)(2,1)} %get-tuple-element.22.v_ref), custom_call_target="tpu_custom_call" | custom-call | flops 2147483648 | bytes 3145728 | tf_op jit(solution)/shard_map/self/pallas_call | solution.py:151
  35.4 1.4 copy-done.3
  36.7 3.9 %all-to-all-done = bf16[4,16,32,256]{3,2,1,0:T(8,128)(2,1)} async-done(((bf16[4,16,32,256]{3,2,1,0:T(8,128)(2,1)}), bf16[4,16,32,256]{3,2,1,0:T(8,128)(2,1)}, u32[]{:S(2)}, u32[]{:S(2)}) %all-to-all-start) | async-done | bytes 1048608 | tf_op jit(solution)/shard_map/all_to_all | solution.py:346
  40.6 2.0 %collective-permute-start = (bf16[64,32,256]{2,1,0:T(8,128)(2,1)}, bf16[64,32,256]{2,1,0:T(8,128)(2,1)}, u32[]{:S(2)}, u32[]{:S(2)}) collective-permute-start(bf16[64,32,256]{2,1,0:T(8,128)(2,1)} %bitcast.refs_0_), channel_id=1, source_target_pairs={{0,4},{4,8},{8,12},{12,16},{16,20},{20,24},{24,28},{28,0},{1,5},{5... | collective-permute-start | bytes 3145736 | tf_op jit(solution)/shard_map/ppermute | solution.py:366
  42.9 1.5 broadcast_in_dim.106
  44.3 3.5 %all-to-all-start.2 = ((bf16[4,8,4,4096]{3,2,1,0:T(4,128)(2,1)}), bf16[4,8,4,4096]{3,2,1,0:T(4,128)(2,1)S(1)}, u32[]{:S(2)}, u32[]{:S(2)}) async-start(bf16[4,8,4,4096]{3,2,1,0:T(4,128)(2,1)} %broadcast_in_dim.106), calls=%async_computation.2 | async-start | bytes 2097152 | tf_op jit(solution)/shard_map/all_to_all | solution.py:291
  48.7 10.7 %all-to-all-done.2.xyz_ref = bf16[4,8,4,4096]{3,2,1,0:T(4,128)(2,1)S(1)} async-done(((bf16[4,8,4,4096]{3,2,1,0:T(4,128)(2,1)}), bf16[4,8,4,4096]{3,2,1,0:T(4,128)(2,1)S(1)}, u32[]{:S(2)}, u32[]{:S(2)}) %all-to-all-start.2) | async-done | bytes 1048608 | tf_op jit(solution)/shard_map/all_to_all | solution.py:291
  59.4 7.6 %augment.1 = (bf16[8,64,16,256]{3,2,1,0:T(8,128)(2,1)S(1)}, bf16[64,16,256]{2,1,0:T(8,128)(2,1)S(1)}) custom-call(s32[1]{0:T(128)} %bitcast.6.z_ref, f32[1]{0:T(128)} %bitcast.7.c_ref, bf16[4,8,4,4096]{3,2,1,0:T(4,128)(2,1)S(1)} %all-to-all-done.2.xyz_ref), custom_call_target="tpu_custom_call" | custom-call | tf_op jit(solution)/shard_map/augment/pallas_call | solution.py:112
  67.0 1.9 %copy-done.1 = bf16[8,64,16,256]{3,2,1,0:T(8,128)(2,1)} copy-done((bf16[8,64,16,256]{3,2,1,0:T(8,128)(2,1)}, bf16[8,64,16,256]{3,2,1,0:T(8,128)(2,1)S(1)}, u32[]{:S(2)}) %copy-start.1) | copy-done | bytes 4194328
  69.0 4.9 %near.5.refs_4_ = f32[65,32,256]{2,1,0:T(8,128)S(1)} custom-call(s32[9]{0:T(128)S(1)} %get-tuple-element.40.cnt, s32[9,64]{1,0:T(8,128)S(1)} %fusion.52.lst, bf16[64,16,256]{2,1,0:T(8,128)(2,1)S(1)} %get-tuple-element.25.dst_ref, bf16[64,32,256]{2,1,0:T(8,128)(2,1)} %bitcast.refs_0_, bf16[8,64,16,256]{3,2,1,0:T(8,128)(2,1)} %copy-done.1), custom_call_target="tpu_custom_call" | custom-call | flops 1207959552 | bytes 8388608 | tf_op jit(solution)/shard_map/near/pallas_call | solution.py:212
  73.9 2.0 %collective-permute-start.2 = (bf16[64,32,256]{2,1,0:T(8,128)(2,1)}, bf16[64,32,256]{2,1,0:T(8,128)(2,1)}, u32[]{:S(2)}, u32[]{:S(2)}) collective-permute-start(bf16[64,32,256]{2,1,0:T(8,128)(2,1)} %collective-permute-done.refs_0_), channel_id=1, source_target_pairs={{0,4},{4,8},{8,12},{12,16},{16,20},{20,24},{24,28},{28,0},{1,5},{5... | collective-permute-start | bytes 3145736 | tf_op jit(solution)/shard_map/ppermute | solution.py:366
  75.9 1.3 collective-permute-start.3
  78.2 6.8 %all-to-all-start.4 = ((bf16[32,16,256]{2,1,0:T(8,128)(2,1)}), bf16[32,16,256]{2,1,0:T(8,128)(2,1)S(1)}, u32[]{:S(2)}, u32[]{:S(2)}) async-start(bf16[32,16,256]{2,1,0:T(8,128)(2,1)} %copy.29), calls=%async_computation.4 | async-start | bytes 524288 | tf_op jit(solution)/shard_map/all_to_all | solution.py:300
  86.0 18.1 %all-to-all-done.4 = bf16[32,16,256]{2,1,0:T(8,128)(2,1)S(1)} async-done(((bf16[32,16,256]{2,1,0:T(8,128)(2,1)}), bf16[32,16,256]{2,1,0:T(8,128)(2,1)S(1)}, u32[]{:S(2)}, u32[]{:S(2)}) %all-to-all-start.4) | async-done | bytes 262176 | tf_op jit(solution)/shard_map/all_to_all | solution.py:300
  104.3 8.6 %near.6.refs_4_ = f32[65,32,256]{2,1,0:T(8,128)S(1)} custom-call(s32[9]{0:T(128)S(1)} %get-tuple-element.40.cnt, s32[9,64]{1,0:T(8,128)S(1)} %fusion.52.lst, bf16[64,16,256]{2,1,0:T(8,128)(2,1)S(1)} %get-tuple-element.25.dst_ref, bf16[64,32,256]{2,1,0:T(8,128)(2,1)} %collective-permute-done.refs_0_, ...), custom_call_target="tpu_custom_call", output_to_operand_aliasing={{}: (7, {})} | custom-call | flops 2415919104 | bytes 8388608 | tf_op jit(solution)/shard_map/near/pallas_call | solution.py:212
  112.9 4.9 %collective-permute-start.4 = (bf16[64,32,256]{2,1,0:T(8,128)(2,1)}, bf16[64,32,256]{2,1,0:T(8,128)(2,1)}, u32[]{:S(2)}, u32[]{:S(2)}) collective-permute-start(bf16[64,32,256]{2,1,0:T(8,128)(2,1)} %collective-permute-done.2.refs_0_), channel_id=1, source_target_pairs={{0,4},{4,8},{8,12},{12,16},{16,20},{20,24},{24,28},{28,0},{1,5},{5... | collective-permute-start | bytes 3145736 | tf_op jit(solution)/shard_map/ppermute | solution.py:366
  118.8 4.5 %all-to-all-start.5 = ((bf16[8,8,256]{2,1,0:T(8,128)(2,1)}), bf16[8,8,256]{2,1,0:T(8,128)(2,1)S(1)}, u32[]{:S(2)}, u32[]{:S(2)}) async-start(bf16[8,8,256]{2,1,0:T(8,128)(2,1)} %broadcast_in_dim.107), calls=%async_computation.5 | async-start | bytes 65536 | tf_op jit(solution)/shard_map/all_to_all | solution.py:291
  123.6 3.2 %all-to-all-done.5 = bf16[8,8,256]{2,1,0:T(8,128)(2,1)S(1)} async-done(((bf16[8,8,256]{2,1,0:T(8,128)(2,1)}), bf16[8,8,256]{2,1,0:T(8,128)(2,1)S(1)}, u32[]{:S(2)}, u32[]{:S(2)}) %all-to-all-start.5) | async-done | bytes 32800 | tf_op jit(solution)/shard_map/all_to_all | solution.py:291
  127.6 8.6 %near.7.refs_4_ = f32[65,32,256]{2,1,0:T(8,128)S(1)} custom-call(s32[9]{0:T(128)S(1)} %get-tuple-element.40.cnt, s32[9,64]{1,0:T(8,128)S(1)} %fusion.52.lst, bf16[64,16,256]{2,1,0:T(8,128)(2,1)S(1)} %get-tuple-element.25.dst_ref, bf16[64,32,256]{2,1,0:T(8,128)(2,1)} %collective-permute-done.2.refs_0_, ...), custom_call_target="tpu_custom_call", output_to_operand_aliasing={{}: (7, {})} | custom-call | flops 2415919104 | bytes 8388608 | tf_op jit(solution)/shard_map/near/pallas_call | solution.py:212
  136.6 1.9 slice.20
  138.5 1.9 slice.19
  140.4 3.3 %collective-permute-start.6 = (bf16[32,32,256]{2,1,0:T(8,128)(2,1)}, bf16[32,32,256]{2,1,0:T(8,128)(2,1)S(1)}, u32[]{:S(2)}, u32[]{:S(2)}) collective-permute-start(bf16[32,32,256]{2,1,0:T(8,128)(2,1)} %slice.19), channel_id=1, source_target_pairs={{0,4},{4,8},{8,12},{12,16},{16,20},{20,24},{24,28},{28,0},{1,5},{5... | collective-permute-start | bytes 1572872 | tf_op jit(solution)/shard_map/ppermute | solution.py:371
  145.0 9.4 %all-to-all-start.6 = ((bf16[32,16,256]{2,1,0:T(8,128)(2,1)}), bf16[32,16,256]{2,1,0:T(8,128)(2,1)S(1)}, u32[]{:S(2)}, u32[]{:S(2)}) async-start(bf16[32,16,256]{2,1,0:T(8,128)(2,1)} %bitcast.45), calls=%async_computation.6 | async-start | bytes 524288 | tf_op jit(solution)/shard_map/all_to_all | solution.py:323
  154.4 8.6 %near.8.refs_4_ = f32[65,32,256]{2,1,0:T(8,128)S(1)} custom-call(s32[9]{0:T(128)S(1)} %get-tuple-element.40.cnt, s32[9,64]{1,0:T(8,128)S(1)} %fusion.52.lst, bf16[64,16,256]{2,1,0:T(8,128)(2,1)S(1)} %get-tuple-element.25.dst_ref, bf16[64,32,256]{2,1,0:T(8,128)(2,1)} %collective-permute-done.4.refs_0_, ...), custom_call_target="tpu_custom_call", output_to_operand_aliasing={{}: (7, {})} | custom-call | flops 2415919104 | bytes 8388608 | tf_op jit(solution)/shard_map/near/pallas_call | solution.py:212
  163.0 4.9 %near.9 = (f32[65,32,256]{2,1,0:T(8,128)S(1)}, bf16[64,32,256]{2,1,0:T(8,128)(2,1)S(1)}) custom-call(s32[9]{0:T(128)S(1)} %get-tuple-element.40.cnt, s32[9,64]{1,0:T(8,128)S(1)} %fusion.52.lst, bf16[64,16,256]{2,1,0:T(8,128)(2,1)S(1)} %get-tuple-element.25.dst_ref, ...), custom_call_target="tpu_custom_call", output_to_operand_aliasing={{0}: (7, {})} | custom-call | flops 2415919104 | bytes 8388608 | tf_op jit(solution)/shard_map/near/pallas_call | solution.py:212
  168.9 4.7 %all-to-all-start.3 = ((bf16[4,16,32,256]{3,2,1,0:T(8,128)(2,1)}), bf16[4,16,32,256]{3,2,1,0:T(8,128)(2,1)S(1)}, u32[]{:S(2)}, u32[]{:S(2)}) async-start(bf16[4,16,32,256]{3,2,1,0:T(8,128)(2,1)} %bitcast.40), calls=%async_computation.3 | async-start | bytes 2097152 | tf_op jit(solution)/shard_map/all_to_all | solution.py:374
  176.4 12.9 %all-to-all-done.3.near_ref = bf16[4,16,32,256]{3,2,1,0:T(8,128)(2,1)S(1)} async-done(((bf16[4,16,32,256]{3,2,1,0:T(8,128)(2,1)}), bf16[4,16,32,256]{3,2,1,0:T(8,128)(2,1)S(1)}, u32[]{:S(2)}, u32[]{:S(2)}) %all-to-all-start.3) | async-done | bytes 1048608 | tf_op jit(solution)/shard_map/all_to_all | solution.py:374
  189.3 3.2 %final.1 = bf16[4096,128]{1,0:T(8,128)(2,1)} custom-call(f32[4,16,32,256]{3,2,1,0:T(8,128)S(1)} %copy-done.4, bf16[4,16,32,256]{3,2,1,0:T(8,128)(2,1)S(1)} %all-to-all-done.3.near_ref, bf16[16,64,128]{2,1,0:T(8,128)(2,1)S(1)} %bitcast.39, bf16[256,64]{1,0:T(8,128)(2,1)S(1)} %copy.28.ex_ref, bf16[128,128]{1,0:T(8,128)(2,1)S(1)} %copy-done.7), custom_call_target="tpu_custom_call" | custom-call | tf_op jit(solution)/shard_map/final/pallas_call | solution.py:272
  (81 shorter events, 17.5 us)
Async XLA Ops:
  0.0 117.9 %copy-start = (bf16[128,128]{1,0:T(8,128)(2,1)S(1)}, bf16[128,128]{1,0:T(8,128)(2,1)}, u32[]{:S(2)}) copy-start(bf16[128,128]{1,0:T(8,128)(2,1)} %param.22) | copy-start | bytes 98308
  0.7 26.7 %copy-start.14 = (f32[4]{0:T(128)S(1)}, f32[4]{0:T(128)}, u32[]{:S(2)}) copy-start(f32[4]{0:T(128)} %param.19) | copy-start | bytes 52
  0.7 27.3 %copy-start.10 = (bf16[3,4096]{1,0:T(4,128)(2,1)S(1)}, bf16[3,4096]{1,0:T(4,128)(2,1)}, u32[]{:S(2)}) copy-start(bf16[3,4096]{1,0:T(4,128)(2,1)} %xyz_ref.1) | copy-start | bytes 73732
  2.3 20.3 %all-to-all-start.1 = ((bf16[8,4,4096]{2,1,0:T(4,128)(2,1)}), bf16[8,4,4096]{2,1,0:T(4,128)(2,1)S(1)}, u32[]{:S(2)}, u32[]{:S(2)}) async-start(bf16[8,4,4096]{2,1,0:T(4,128)(2,1)} %broadcast_in_dim.95), calls=%async_computation.1 | async-start | bytes 524288 | tf_op jit(solution)/shard_map/all_to_all | solution.py:291
  10.8 1.2 copy-start.5
  12.0 0.8 copy-start.8
  12.8 0.8 copy-start.9
  22.7 17.9 %all-to-all-start = ((bf16[4,16,32,256]{3,2,1,0:T(8,128)(2,1)}), bf16[4,16,32,256]{3,2,1,0:T(8,128)(2,1)}, u32[]{:S(2)}, u32[]{:S(2)}) async-start(bf16[4,16,32,256]{3,2,1,0:T(8,128)(2,1)} %get-tuple-element.22.v_ref), calls=%async_computation | async-start | bytes 2097152 | tf_op jit(solution)/shard_map/all_to_all | solution.py:346
  35.4 1.4 copy-start.3
  40.6 33.3 %collective-permute-start.1 = (bf16[64,32,256]{2,1,0:T(8,128)(2,1)}, bf16[64,32,256]{2,1,0:T(8,128)(2,1)}, u32[]{:S(2)}, u32[]{:S(2)}) collective-permute-start(bf16[64,32,256]{2,1,0:T(8,128)(2,1)} %bitcast.refs_0_), channel_id=1, source_target_pairs={{0,28},{4,0},{8,4},{12,8},{16,12},{20,16},{24,20},{28,24},{1,29},{... | collective-permute-start | bytes 3145736 | tf_op jit(solution)/shard_map/ppermute | solution.py:367
  40.6 33.3 %collective-permute-start = (bf16[64,32,256]{2,1,0:T(8,128)(2,1)}, bf16[64,32,256]{2,1,0:T(8,128)(2,1)}, u32[]{:S(2)}, u32[]{:S(2)}) collective-permute-start(bf16[64,32,256]{2,1,0:T(8,128)(2,1)} %bitcast.refs_0_), channel_id=1, source_target_pairs={{0,4},{4,8},{8,12},{12,16},{16,20},{20,24},{24,28},{28,0},{1,5},{5... | collective-permute-start | bytes 3145736 | tf_op jit(solution)/shard_map/ppermute | solution.py:366
  44.3 15.1 %all-to-all-start.2 = ((bf16[4,8,4,4096]{3,2,1,0:T(4,128)(2,1)}), bf16[4,8,4,4096]{3,2,1,0:T(4,128)(2,1)S(1)}, u32[]{:S(2)}, u32[]{:S(2)}) async-start(bf16[4,8,4,4096]{3,2,1,0:T(4,128)(2,1)} %broadcast_in_dim.106), calls=%async_computation.2 | async-start | bytes 2097152 | tf_op jit(solution)/shard_map/all_to_all | solution.py:291
  59.4 9.6 %copy-start.2 = (bf16[4,8,4,4096]{3,2,1,0:T(4,128)(2,1)}, bf16[4,8,4,4096]{3,2,1,0:T(4,128)(2,1)S(1)}, u32[]{:S(2)}) copy-start(bf16[4,8,4,4096]{3,2,1,0:T(4,128)(2,1)S(1)} %all-to-all-done.2.xyz_ref) | copy-start | bytes 3145732
  67.0 2.0 %copy-start.1 = (bf16[8,64,16,256]{3,2,1,0:T(8,128)(2,1)}, bf16[8,64,16,256]{3,2,1,0:T(8,128)(2,1)S(1)}, u32[]{:S(2)}) copy-start(bf16[8,64,16,256]{3,2,1,0:T(8,128)(2,1)S(1)} %get-tuple-element.27.refs_1_.refs_2_.refs_3_) | copy-start | bytes 12582916
  73.9 39.1 %collective-permute-start.2 = (bf16[64,32,256]{2,1,0:T(8,128)(2,1)}, bf16[64,32,256]{2,1,0:T(8,128)(2,1)}, u32[]{:S(2)}, u32[]{:S(2)}) collective-permute-start(bf16[64,32,256]{2,1,0:T(8,128)(2,1)} %collective-permute-done.refs_0_), channel_id=1, source_target_pairs={{0,4},{4,8},{8,12},{12,16},{16,20},{20,24},{24,28},{28,0},{1,5},{5... | collective-permute-start | bytes 3145736 | tf_op jit(solution)/shard_map/ppermute | solution.py:366
  75.9 37.0 %collective-permute-start.3 = (bf16[64,32,256]{2,1,0:T(8,128)(2,1)}, bf16[64,32,256]{2,1,0:T(8,128)(2,1)}, u32[]{:S(2)}, u32[]{:S(2)}) collective-permute-start(bf16[64,32,256]{2,1,0:T(8,128)(2,1)} %collective-permute-done.1.refs_1_), channel_id=1, source_target_pairs={{0,28},{4,0},{8,4},{12,8},{16,12},{20,16},{24,20},{28,24},{1,29},{... | collective-permute-start | bytes 3145736 | tf_op jit(solution)/shard_map/ppermute | solution.py:367
  78.2 25.8 %all-to-all-start.4 = ((bf16[32,16,256]{2,1,0:T(8,128)(2,1)}), bf16[32,16,256]{2,1,0:T(8,128)(2,1)S(1)}, u32[]{:S(2)}, u32[]{:S(2)}) async-start(bf16[32,16,256]{2,1,0:T(8,128)(2,1)} %copy.29), calls=%async_computation.4 | async-start | bytes 524288 | tf_op jit(solution)/shard_map/all_to_all | solution.py:300
  104.3 13.8 %copy-start.13 = (s32[128]{0:T(128)S(1)}, s32[128]{0:T(128)}, u32[]{:S(2)}) copy-start(s32[128]{0:T(128)} %param.18) | copy-start | bytes 1540
  104.3 19.1 %copy-start.11 = (bf16[128,128]{1,0:T(8,128)(2,1)S(1)}, bf16[128,128]{1,0:T(8,128)(2,1)}, u32[]{:S(2)}) copy-start(bf16[128,128]{1,0:T(8,128)(2,1)} %param.24) | copy-start | bytes 98308
  112.9 23.2 %collective-permute-start.4 = (bf16[64,32,256]{2,1,0:T(8,128)(2,1)}, bf16[64,32,256]{2,1,0:T(8,128)(2,1)}, u32[]{:S(2)}, u32[]{:S(2)}) collective-permute-start(bf16[64,32,256]{2,1,0:T(8,128)(2,1)} %collective-permute-done.2.refs_0_), channel_id=1, source_target_pairs={{0,4},{4,8},{8,12},{12,16},{16,20},{20,24},{24,28},{28,0},{1,5},{5... | collective-permute-start | bytes 3145736 | tf_op jit(solution)/shard_map/ppermute | solution.py:366
  117.8 18.8 %collective-permute-start.5 = (bf16[64,32,256]{2,1,0:T(8,128)(2,1)}, bf16[64,32,256]{2,1,0:T(8,128)(2,1)}, u32[]{:S(2)}, u32[]{:S(2)}) collective-permute-start(bf16[64,32,256]{2,1,0:T(8,128)(2,1)} %collective-permute-done.3.refs_1_), channel_id=1, source_target_pairs={{0,28},{4,0},{8,4},{12,8},{16,12},{20,16},{24,20},{28,24},{1,29},{... | collective-permute-start | bytes 3145736 | tf_op jit(solution)/shard_map/ppermute | solution.py:367
  118.8 7.9 %all-to-all-start.5 = ((bf16[8,8,256]{2,1,0:T(8,128)(2,1)}), bf16[8,8,256]{2,1,0:T(8,128)(2,1)S(1)}, u32[]{:S(2)}, u32[]{:S(2)}) async-start(bf16[8,8,256]{2,1,0:T(8,128)(2,1)} %broadcast_in_dim.107), calls=%async_computation.5 | async-start | bytes 65536 | tf_op jit(solution)/shard_map/all_to_all | solution.py:291
  127.5 16.1 %copy-start.12 = (bf16[128,128]{1,0:T(8,128)(2,1)S(1)}, bf16[128,128]{1,0:T(8,128)(2,1)}, u32[]{:S(2)}) copy-start(bf16[128,128]{1,0:T(8,128)(2,1)} %param.23) | copy-start | bytes 98308
  140.4 22.6 %collective-permute-start.6 = (bf16[32,32,256]{2,1,0:T(8,128)(2,1)}, bf16[32,32,256]{2,1,0:T(8,128)(2,1)S(1)}, u32[]{:S(2)}, u32[]{:S(2)}) collective-permute-start(bf16[32,32,256]{2,1,0:T(8,128)(2,1)} %slice.19), channel_id=1, source_target_pairs={{0,4},{4,8},{8,12},{12,16},{16,20},{20,24},{24,28},{28,0},{1,5},{5... | collective-permute-start | bytes 1572872 | tf_op jit(solution)/shard_map/ppermute | solution.py:371
  143.7 19.3 %collective-permute-start.7 = (bf16[32,32,256]{2,1,0:T(8,128)(2,1)}, bf16[32,32,256]{2,1,0:T(8,128)(2,1)}, u32[]{:S(2)}, u32[]{:S(2)}) collective-permute-start(bf16[32,32,256]{2,1,0:T(8,128)(2,1)} %slice.20), channel_id=1, source_target_pairs={{0,28},{4,0},{8,4},{12,8},{16,12},{20,16},{24,20},{28,24},{1,29},{... | collective-permute-start | bytes 1572872 | tf_op jit(solution)/shard_map/ppermute | solution.py:372
  145.0 23.9 %all-to-all-start.6 = ((bf16[32,16,256]{2,1,0:T(8,128)(2,1)}), bf16[32,16,256]{2,1,0:T(8,128)(2,1)S(1)}, u32[]{:S(2)}, u32[]{:S(2)}) async-start(bf16[32,16,256]{2,1,0:T(8,128)(2,1)} %bitcast.45), calls=%async_computation.6 | async-start | bytes 524288 | tf_op jit(solution)/shard_map/all_to_all | solution.py:323
  167.9 1.0 copy-start.6
  168.9 20.5 %copy-start.4 = (f32[4,16,32,256]{3,2,1,0:T(8,128)S(1)}, f32[4,16,32,256]{3,2,1,0:T(8,128)}, u32[]{:S(2)}) copy-start(f32[4,16,32,256]{3,2,1,0:T(8,128)} %copy-done.3) | copy-start | bytes 6291460
  168.9 20.5 %copy-start.7 = (bf16[128,128]{1,0:T(8,128)(2,1)S(1)}, bf16[128,128]{1,0:T(8,128)(2,1)}, u32[]{:S(2)}) copy-start(bf16[128,128]{1,0:T(8,128)(2,1)} %wo_ref.1) | copy-start | bytes 98308
  168.9 20.4 %all-to-all-start.3 = ((bf16[4,16,32,256]{3,2,1,0:T(8,128)(2,1)}), bf16[4,16,32,256]{3,2,1,0:T(8,128)(2,1)S(1)}, u32[]{:S(2)}, u32[]{:S(2)}) async-start(bf16[4,16,32,256]{3,2,1,0:T(8,128)(2,1)} %bitcast.40), calls=%async_computation.3 | async-start | bytes 2097152 | tf_op jit(solution)/shard_map/all_to_all | solution.py:374
